TPU v7x, 256 devices: a whole 4x4x8 slice. The times are simulated.
256 devices in a mesh: row: 8 (over y, x_hi), pair: 32 (over z, x_lo, core).
Axes of the slice: x: 4 (x_hi: 2, x_lo: 2; x = x_hi * 2 + x_lo), y: 4, z: 8, core: 2. Of those that a mesh axis runs over, the one named last changes fastest.
Arguments:
- top_blocks: float32 [16384, 8192], P('row', 'pair'), may hold values from -60 to 60, as said below
- bottom_blocks: float32 [16384, 8192], P('row', 'pair'), may hold values from -60 to 60, as said below
Outputs:
- top_out: float32 [16384, 8192], P('row', 'pair')
- bottom_out: float32 [16384, 8192], P('row', 'pair')
Inputs may be any that keep to these rules, and one draw needn't show every extreme that they name: `top_blocks`: entries of the slab. `bottom_blocks`: entries of the slab.
All inputs are finite; a program needn't handle non-finite values.
Results may differ from a plain program's by a relative error of at most 0.00015.
Values sent between devices are 32-bit elements; how exact they have to be, the bound alone decides.
No kernel may reach another device: no remote copies, remote signals or barrier semaphores. Data moves between devices by JAX's collectives and lax.ppermute only.
A program may use at most 64 MiB of HBM per device.

v0:
```python
import jax
import jax.numpy as jnp
from jax import lax
from jax.sharding import PartitionSpec as P

STEPS = 2
SWEEPS = 3


def passed_along(array, axis, by):
    length = lax.axis_size(axis)
    return lax.ppermute(array, axis, [(i, (i + by) % length) for i in range(length)])


def matmul_hi(left, right):
    return jnp.dot(left, right, preferred_element_type=jnp.float32, precision=lax.Precision.HIGHEST)


def rotation(gram_mat):
    width_n = gram_mat.shape[0]
    col_sq = jnp.diagonal(gram_mat) + 1e-06
    corr_mat = gram_mat / jnp.sqrt(col_sq[:, None] * col_sq[None, :])
    skew_mat = (col_sq[None, :] - col_sq[:, None]) / (col_sq[None, :] + col_sq[:, None])
    generator = corr_mat * skew_mat
    frobenius = jnp.sqrt(jnp.sum(generator * generator))
    identity = jnp.eye(width_n, dtype=jnp.float32)
    rotate = identity + generator / (1.0 + frobenius)
    for sweep_idx in range(SWEEPS):
        inner_mat = matmul_hi(rotate.T, rotate)
        rotate = matmul_hi(rotate, 1.5 * identity - 0.5 * inner_mat)
    return rotate


def on_device(top_blocks, bottom_blocks):
    width_n = top_blocks.shape[1]
    top_block = top_blocks
    bottom_block = bottom_blocks
    for step_idx in range(STEPS):
        joined = jnp.concatenate([top_block, bottom_block], axis=1)
        gram_mat = lax.psum(matmul_hi(joined.T, joined), "row")
        rotated = matmul_hi(joined, rotation(gram_mat))
        bottom_block = rotated[:, width_n:]
        top_block = passed_along(rotated[:, :width_n], "pair", 1)
    return (top_block, bottom_block)


def solution(mesh):
    placed = (P("row", "pair"), P("row", "pair"))
    return jax.shard_map(
        on_device,
        mesh=mesh,
        in_specs=placed,
        out_specs=(P("row", "pair"), P("row", "pair")),
        check_vma=False,
    )
```

profile of v0, /device:TPU:128, one launch (start us, length us, event | category | flops | bytes accessed | tf_op | source)
XLA Modules:
  0.0 352.7 jit_solution(6922078462349345211)
XLA Ops:
  7.2 2.0 constant_dynamic-update-slice_fusion.1
  9.7 1.9 copy-done
  11.6 8.0 %fusion.8 = f32[512,512]{1,0:T(8,128)} fusion(f32[2048,512]{1,0:T(8,128)S(1)} %constant_dynamic-update-slice_fusion), kind=kOutput, calls=%fused_computation.35 | convolution fusion | flops 6442450944 | bytes 5242880 | tf_op jit(solution)/shard_map/dot_general | solution.py:16
  19.7 97.6 %all-reduce.3.cloned.1.call-done = f32[512,512]{1,0:T(8,128)} async-done(((f32[512,512]{1,0:T(8,128)}), f32[512,512]{1,0:T(8,128)}) %all-reduce.3.cloned.1.call-update) | async-done | bytes 1048592 | tf_op jit(solution)/shard_map/psum | solution.py:40
  117.3 8.7 %gather_fusion = f32[512]{0:T(512)S(1)} fusion(f32[512,512]{1,0:T(8,128)} %all-reduce.3.cloned.1.call-done, s32[512]{0:T(512)S(1)} %bitcast.24), kind=kCustom, calls=%fused_computation | custom fusion | bytes 8192 | tf_op jit(solution)/shard_map/jit(diagonal)/cond/branch_0_fun/gather | solution.py:21
  126.0 2.3 multiply_reduce_fusion.1
  129.1 4.3 %select_subtract_fusion.5 = f32[512,512]{1,0:T(8,128)S(1)} fusion(f32[]{:T(128)S(6)} %add.64, f32[512,512]{1,0:T(8,128)} %all-reduce.3.cloned.1.call-done, f32[512]{0:T(512)S(1)} %broadcast_add_fusion.1), kind=kOutput, calls=%fused_computation.10 | convolution fusion | flops 1614282752 | bytes 2099204 | tf_op jit(solution)/shard_map/dot_general | solution.py:16
  133.4 2.2 fusion.2
  135.6 1.9 select_subtract_fusion.4
  139.3 1.9 select_subtract_fusion.3
  141.2 2.3 fusion.10
  143.5 7.0 %fusion.11 = f32[2048,512]{0,1:T(8,128)S(1)} fusion(f32[2048,512]{1,0:T(8,128)S(1)} %copy-done.1, f32[512,512]{1,0:T(8,128)S(1)} %fusion.10), kind=kOutput, calls=%fused_computation.38 | convolution fusion | flops 6442450944 | bytes 9437184 | tf_op jit(solution)/shard_map/dot_general | solution.py:16
  151.2 27.6 %collective-permute-done = f32[2048,256]{0,1:T(8,128)S(1)} collective-permute-done((f32[2048,256]{0,1:T(8,128)S(1)}, f32[2048,256]{0,1:T(8,128)S(1)}, u32[]{:S(2)}, u32[]{:S(2)}) %collective-permute-start) | collective-permute-done | bytes 2097184 | tf_op jit(solution)/shard_map/ppermute | solution.py:12
  180.1 7.9 %fusion.1 = f32[512,512]{1,0:T(8,128)} fusion(f32[2048,256]{0,1:T(8,128)S(1)} %get-tuple-element.5, f32[2048,256]{0,1:T(8,128)S(1)} %collective-permute-done), kind=kOutput, calls=%fused_computation.4 | convolution fusion | flops 6443499520 | bytes 5242880 | tf_op jit(solution)/shard_map/dot_general | solution.py:16
  188.0 93.8 %all-reduce.5.cloned.1.call-done = f32[512,512]{1,0:T(8,128)} async-done(((f32[512,512]{1,0:T(8,128)}), f32[512,512]{1,0:T(8,128)}) %all-reduce.5.cloned.1.call-update) | async-done | bytes 1048592 | tf_op jit(solution)/shard_map/psum | solution.py:40
  281.8 8.8 %gather_fusion.1 = f32[512]{0:T(512)S(1)} fusion(f32[512,512]{1,0:T(8,128)} %all-reduce.5.cloned.1.call-done, s32[512]{0:T(512)S(1)} %bitcast.25), kind=kCustom, calls=%fused_computation.1 | custom fusion | bytes 8192 | tf_op jit(solution)/shard_map/jit(diagonal)/cond/branch_0_fun/gather | solution.py:21
  290.6 2.3 multiply_reduce_fusion
  293.7 4.3 %select_subtract_fusion.2 = f32[512,512]{1,0:T(8,128)S(1)} fusion(f32[]{:T(128)S(6)} %add.68, f32[512,512]{1,0:T(8,128)} %all-reduce.5.cloned.1.call-done, f32[512]{0:T(512)S(1)} %broadcast_add_fusion), kind=kOutput, calls=%fused_computation.7 | convolution fusion | flops 1614282752 | bytes 2099204 | tf_op jit(solution)/shard_map/dot_general | solution.py:16
  298.0 2.2 fusion.3
  300.2 1.9 select_subtract_fusion.1
  303.9 1.9 select_subtract_fusion
  305.8 2.1 fusion.13
  307.9 7.0 %fusion = f32[2048,512]{1,0:T(8,128)S(1)} fusion(f32[512,512]{1,0:T(8,128)S(1)} %fusion.13, f32[2048,256]{0,1:T(8,128)S(1)} %get-tuple-element.5, f32[2048,256]{0,1:T(8,128)S(1)} %copy-done.6), kind=kOutput, calls=%fused_computation.3 | convolution fusion | flops 6443499520 | bytes 9437184 | tf_op jit(solution)/shard_map/dot_general | solution.py:16
  316.6 27.6 %collective-permute-done.1 = f32[2048,256]{1,0:T(8,128)S(1)} collective-permute-done((f32[2048,256]{1,0:T(8,128)S(1)}, f32[2048,256]{1,0:T(8,128)S(1)}, u32[]{:S(2)}, u32[]{:S(2)}) %collective-permute-start.1) | collective-permute-done | bytes 2097184 | tf_op jit(solution)/shard_map/ppermute | solution.py:12
  (28 shorter events, 9.3 us)
Async XLA Ops:
  7.2 2.2 copy-start.4
  7.2 110.2 %all-reduce.3.cloned.1.call-start = ((), (), s32[]{:S(2)}) async-start(), calls=%async_computation | async-start | bytes 2097152 | tf_op jit(solution)/shard_map/psum | solution.py:40
  9.6 1.9 copy-start
  19.6 262.2 %all-reduce.5.cloned.1.call-start = ((), (), s32[]{:S(2)}) async-start(), calls=%async_computation.1 | async-start | bytes 2097152 | tf_op jit(solution)/shard_map/psum | solution.py:40
  129.0 4.3 %copy-start.2 = (f32[512,512]{1,0:T(8,128)S(1)}, f32[512,512]{1,0:T(8,128)}, u32[]{:S(2)}) copy-start(f32[512,512]{1,0:T(8,128)} %all-reduce.3.cloned.1.call-done) | copy-start | bytes 3145732
  137.5 6.0 %copy-start.1 = (f32[2048,512]{1,0:T(8,128)S(1)}, f32[2048,512]{1,0:T(8,128)}, u32[]{:S(2)}) copy-start(f32[2048,512]{1,0:T(8,128)} %copy-done) | copy-start | bytes 12582916
  151.0 27.8 %collective-permute-start = (f32[2048,256]{0,1:T(8,128)S(1)}, f32[2048,256]{0,1:T(8,128)S(1)}, u32[]{:S(2)}, u32[]{:S(2)}) collective-permute-start(f32[2048,256]{0,1:T(8,128)S(1)} %get-tuple-element.4), channel_id=1, source_target_pairs={{0,1},{1,2},{2,3},{3,4},{4,5},{5,6},{6,7},{7,8},{8,9},{9,10},{10,1... | collective-permute-start | bytes 6291464 | tf_op jit(solution)/shard_map/ppermute | solution.py:12
  178.8 1.3 copy-start.5
  293.6 4.3 %copy-start.3 = (f32[512,512]{1,0:T(8,128)S(1)}, f32[512,512]{1,0:T(8,128)}, u32[]{:S(2)}) copy-start(f32[512,512]{1,0:T(8,128)} %all-reduce.5.cloned.1.call-done) | copy-start | bytes 3145732
  302.0 5.9 %copy-start.6 = (f32[2048,256]{0,1:T(8,128)S(1)}, f32[2048,256]{0,1:T(8,128)}, u32[]{:S(2)}) copy-start(f32[2048,256]{0,1:T(8,128)} %copy-done.5) | copy-start | bytes 6291460
  316.6 27.6 %collective-permute-start.1 = (f32[2048,256]{1,0:T(8,128)S(1)}, f32[2048,256]{1,0:T(8,128)S(1)}, u32[]{:S(2)}, u32[]{:S(2)}) collective-permute-start(f32[2048,256]{1,0:T(8,128)S(1)} %get-tuple-element.3), channel_id=1, source_target_pairs={{0,1},{1,2},{2,3},{3,4},{4,5},{5,6},{6,7},{7,8},{8,9},{9,10},{10,1... | collective-permute-start | bytes 6291464 | tf_op jit(solution)/shard_map/ppermute | solution.py:12
Sparse Core Ops, SparseCore 0:
  19.7 97.5 all-reduce.2
  188.1 93.5 all-reduce.4
where the time goes:
time: 359 us; the launch traced here: 353 us
  waiting for transfers between devices  247 us (69%)
  matrix products  58.4 us (16%)
  local copies, waits for them, and re-layouts  26.7 us (7%)
  between operations  16.1 us (4%)
  other arithmetic  4.66 us (1%)
    psum x2, waiting for transfers between devices, on_device(): gram_mat = lax.psum(matmul_hi(joined.T, joined), 'row')  191 us
    dot_general x16, matrix products, matmul_hi(): jnp.dot(left, right, preferred_element_type=jnp.float32, precision=lax.Pr...  58.4 us
    ppermute x2, waiting for transfers between devices, passed_along(): lax.ppermute(array, axis, [(i, (i + by) % length) for i in range(length)])  55.1 us
    gather x2, local copies, waits for them, and re-layouts, rotation(): col_sq = jnp.diagonal(gram_mat) + 1e-06  17.5 us
  transfers between devices with their start and end apart: 4, of which 4 were waited for; matrix products, arithmetic and copies ran while one was open for 0% of the time, Pallas kernels for 0%

commit v1 on v0

v1 whole, which is shorter than its diff:
```python
import functools

import jax
import jax.numpy as jnp
from jax import lax
from jax.experimental import pallas as pl
from jax.experimental.pallas import tpu as pltpu
from jax.sharding import PartitionSpec as P

STEPS = 2
SWEEPS = 3
W = 256
H = 128
PIECE = 2 * H + 8
CHUNK = 512
BF, F32 = jnp.bfloat16, jnp.float32
VMEM_LIMIT = 48 * 1024 * 1024


def split2(x):
    high = x.astype(BF)
    return high, (x - high.astype(F32)).astype(BF)


def dot_tn(left, right):
    return lax.dot_general(left, right, (((0,), (0,)), ((), ())), preferred_element_type=F32)


def dot_nn(left, right):
    return jnp.dot(left, right, preferred_element_type=F32)


def mm3(left, right):
    lh, ll = left
    rh, rl = right
    return dot_nn(lh, rh) + (dot_nn(lh, rl) + dot_nn(ll, rh))


def mm1(left, right):
    return dot_nn(left[0], right[0])


def iotas(shape):
    return lax.broadcasted_iota(jnp.int32, shape, 0), lax.broadcasted_iota(jnp.int32, shape, 1)


def gram_kernel(where_ref, top_ref, bottom_ref, *refs):
    outs, (xtt, ytt, xbb, ybb, tb, pieces) = refs[:4], refs[4:]
    step = pl.program_id(0)

    @pl.when(step == 0)
    def _():
        for acc in (xtt, ytt, xbb, ybb, tb):
            acc[...] = jnp.zeros_like(acc)

    th, tl = split2(top_ref[...])
    bh, bl = split2(bottom_ref[...])
    xtt[...] += dot_tn(th, th)
    ytt[...] += dot_tn(th, tl)
    xbb[...] += dot_tn(bh, bh)
    ybb[...] += dot_tn(bh, bl)
    tb[...] += dot_tn(th, bh) + (dot_tn(th, bl) + dot_tn(tl, bh))

    @pl.when(step == pl.num_programs(0) - 1)
    def _():
        row, col = iotas((H, H))
        upper, diag = row <= col, row == col
        for idx, (x, y) in enumerate(((xtt, ytt), (xbb, ybb))):
            full = x[...] + (y[...] + y[...].T)
            first, last = full[:H, :H], full[H:, H:]
            pieces[idx, 0:H] = full[:H, H:]
            pieces[idx, H:2 * H] = jnp.where(upper, first, last)
            line = jnp.sum(jnp.where(diag, last, 0.0), axis=0, keepdims=True)
            pieces[idx, 2 * H:PIECE] = jnp.broadcast_to(line, (8, H))
        for idx in range(2):
            half = tb[idx * H:(idx + 1) * H, :]
            pieces[2 + idx, 0:H] = half[:, :H]
            pieces[2 + idx, H:2 * H] = half[:, H:]
            pieces[2 + idx, 2 * H:PIECE] = jnp.zeros((8, H), F32)
        mine = where_ref[0]
        for ahead in range(4):
            outs[ahead][...] = pieces[(mine + ahead) % 4]


def gram_pieces(where, top, bottom):
    rows = top.shape[0]
    piece = jax.ShapeDtypeStruct((PIECE, H), F32)
    square = pltpu.VMEM((W, W), F32)
    return pl.pallas_call(
        gram_kernel,
        out_shape=[piece] * 4,
        grid_spec=pltpu.PrefetchScalarGridSpec(
            num_scalar_prefetch=1,
            grid=(rows // CHUNK,),
            in_specs=[pl.BlockSpec((CHUNK, W), lambda i, *_: (i, 0))] * 2,
            out_specs=[pl.BlockSpec((PIECE, H), lambda i, *_: (0, 0))] * 4,
            scratch_shapes=[square] * 5 + [pltpu.VMEM((4, PIECE, H), F32)],
        ),
        compiler_params=pltpu.CompilerParams(vmem_limit_bytes=VMEM_LIMIT),
        cost_estimate=pl.CostEstimate(flops=7 * 2 * W * W * rows, bytes_accessed=8 * W * rows, transcendentals=0),
    )(where, top, bottom)


def rotation_kernel(where_ref, q0, q1, q2, q3, high_ref, low_ref, pieces, gram):
    mine = where_ref[0]
    for behind, piece in enumerate((q0, q1, q2, q3)):
        pieces[(mine + 4 - behind) % 4] = piece[...]
    row, col = iotas((H, H))
    upper, diag = row <= col, row == col

    def put(i, j, block):
        gram[i * H:(i + 1) * H, j * H:(j + 1) * H] = block

    lines, columns = [], []
    for half in range(2):
        off = pieces[half, 0:H]
        both = pieces[half, H:2 * H]
        line = pieces[half, 2 * H:2 * H + 1]
        turned = both.T
        first = jnp.where(upper, both, turned)
        last = jnp.where(diag, line, jnp.where(upper, turned, both))
        a, b = 2 * half, 2 * half + 1
        put(a, b, off)
        put(b, a, off.T)
        put(a, a, first)
        put(b, b, last)
        for block in (first, last):
            on = jnp.where(diag, block, 0.0)
            lines.append(jnp.sum(on, axis=0, keepdims=True))
            columns.append(jnp.sum(on, axis=1, keepdims=True))
    for i in range(2):
        for j in range(2):
            block = pieces[2 + i, j * H:(j + 1) * H]
            put(i, 2 + j, block)
            put(2 + j, i, block.T)
    sq_line = jnp.concatenate(lines, axis=1) + 1e-06
    sq_col = jnp.concatenate(columns, axis=0) + 1e-06
    generator = gram[...] / jnp.sqrt(sq_col * sq_line) * ((sq_line - sq_col) / (sq_line + sq_col))
    frobenius = jnp.sqrt(jnp.sum(generator * generator))
    skew = generator * (1.0 / (1.0 + frobenius))

    s2 = split2(skew)
    n = -mm3(s2, s2)
    n_2 = split2(n)
    nn = mm3(n_2, n_2)
    d1 = 0.25 * mm3(split2(nn), n_2) - 0.75 * nn
    d1_2 = split2(d1)
    dd = mm1(d1_2, d1_2)
    d2 = 0.25 * mm1(split2(dd), d1_2) - 0.75 * dd
    x = 0.5 * (d1 + d2) - 0.25 * mm1(d1_2, split2(d2))
    y = 0.5 * n + x - 0.5 * mm3(n_2, split2(x))
    row, col = iotas((2 * W, 2 * W))
    rotate = jnp.where(row == col, 1.0, skew) - (y + mm3(s2, split2(y)))
    high, low = split2(rotate)
    high_ref[...] = high
    low_ref[...] = low


def rotation(where, quarters):
    half = jax.ShapeDtypeStruct((2 * W, 2 * W), BF)
    return pl.pallas_call(
        rotation_kernel,
        out_shape=[half, half],
        in_specs=[pl.BlockSpec(memory_space=pltpu.SMEM)] + [pl.BlockSpec(memory_space=pltpu.VMEM)] * 4,
        out_specs=[pl.BlockSpec(memory_space=pltpu.VMEM)] * 2,
        scratch_shapes=[pltpu.VMEM((4, PIECE, H), F32), pltpu.VMEM((2 * W, 2 * W), F32)],
        compiler_params=pltpu.CompilerParams(vmem_limit_bytes=VMEM_LIMIT),
        cost_estimate=pl.CostEstimate(flops=18 * 2 * (2 * W) ** 3, bytes_accessed=2 ** 21, transcendentals=0),
    )(where, *quarters)


def apply_kernel(top_ref, bottom_ref, high_ref, low_ref, out_ref):
    high, low = high_ref[...], low_ref[...]
    top, bottom = split2(top_ref[...]), split2(bottom_ref[...])
    out_ref[...] = mm3(top, (high[:W], low[:W])) + mm3(bottom, (high[W:], low[W:]))


def rotated(top, bottom, rotate, part, start, rows):
    first = start // CHUNK
    block = pl.BlockSpec((CHUNK, W), lambda i: (first + i, 0))
    turn = pl.BlockSpec((2 * W, W), lambda i: (0, part))
    return pl.pallas_call(
        apply_kernel,
        out_shape=jax.ShapeDtypeStruct((rows, W), F32),
        grid=(rows // CHUNK,),
        in_specs=[block, block, turn, turn],
        out_specs=pl.BlockSpec((CHUNK, W), lambda i: (i, 0)),
        compiler_params=pltpu.CompilerParams(vmem_limit_bytes=VMEM_LIMIT),
        cost_estimate=pl.CostEstimate(flops=6 * 2 * W * W * rows, bytes_accessed=12 * W * rows, transcendentals=0),
    )(top, bottom, *rotate)


def passed_along(array, by):
    length = lax.axis_size("pair")
    return lax.ppermute(array, "pair", [(i, (i + by) % length) for i in range(length)])


def along_y(array, by):
    length = lax.axis_size("row") // 2
    return lax.ppermute(
        array, "row", [(2 * y + h, 2 * ((y + by) % length) + h) for y in range(length) for h in range(2)]
    )


def across_x(array):
    return lax.ppermute(array, "row", [(i, i ^ 1) for i in range(lax.axis_size("row"))])


def summed_quarters(pieces):
    total = pieces[0] + along_y(pieces[1], 1) + along_y(pieces[2], 2) + along_y(pieces[3], 3)
    total = total + across_x(total)
    return [total, along_y(total, 1), along_y(total, 2), along_y(total, 3)]


def on_device(top, bottom):
    where = (lax.axis_index("row") // 2).astype(jnp.int32).reshape(1)
    rows = top.shape[0]
    for step_idx in range(STEPS):
        quarters = summed_quarters(gram_pieces(where, top, bottom))
        rotate = rotation(where, quarters)
        if step_idx < STEPS - 1:
            parts = [
                passed_along(rotated(top, bottom, rotate, 0, start, CHUNK), 1) for start in range(0, rows, CHUNK)
            ]
            bottom = rotated(top, bottom, rotate, 1, 0, rows)
            top = jnp.concatenate(parts)
        else:
            sent = passed_along(rotated(top, bottom, rotate, 0, 0, rows), 1)
            bottom = rotated(top, bottom, rotate, 1, 0, rows)
            top = sent
    return (top, bottom)


def solution(mesh):
    placed = (P("row", "pair"), P("row", "pair"))
    return jax.shard_map(on_device, mesh=mesh, in_specs=placed, out_specs=placed, check_vma=False)
```

time: 359 us -> 139 us (0.39); the launches traced: 353 us -> 138 us
  waiting for transfers between devices: 247 us -> 72.1 us
  matrix products: 58.4 us -> 0 us
  Pallas kernels: 0 us -> 33.5 us
  starting transfers between devices: 0.34 us -> 27.1 us
  local copies, waits for them, and re-layouts: 26.7 us -> 4.66 us
  between operations: 16.1 us -> 0.86 us
  other arithmetic: 4.66 us -> 0.13 us
    psum x2 -> x0, waiting for transfers between devices: 191 us -> none  [on_device(): gram_mat = lax.psum(matmul_hi(joined.T, joined), 'row')]
    dot_general x16 -> x0, matrix products: 58.4 us -> none  [matmul_hi(): jnp.dot(left, right, preferred_element_type=jnp.float32, precision=lax.Pr...]
    pallas_call x0 -> x11, Pallas kernels: none -> 33.5 us  [the longest x7 13.8 us: rotated(): pl.pallas_call(apply_kernel, out_shape=jax.ShapeDtypeStruct((rows, W), F3...]
    ppermute x2 -> x19, starting transfers between devices: 0.26 us -> 27.1 us  [the longest x12 17.5 us: along_y(): lax.ppermute(array, 'row', [(2 * y + h, 2 * ((y + by) % length) + h) for...]
    gather x2 -> x0, local copies, waits for them, and re-layouts: 17.5 us -> none  [rotation(): col_sq = jnp.diagonal(gram_mat) + 1e-06]
    ppermute x2 -> x19, waiting for transfers between devices: 55.1 us -> 72.1 us  [the longest x5 42.7 us: passed_along(): lax.ppermute(array, 'pair', [(i, (i + by) % length) for i in range(length)])]
    reduce_sum x2 -> x0, other arithmetic: 4.65 us -> none  [rotation(): frobenius = jnp.sqrt(jnp.sum(generator * generator))]
  transfers between devices with their start and end apart: 4 -> 19, of which waited for: 4 -> 17; matrix products, arithmetic and copies ran while one was open for 0% -> 0% of each run, Pallas kernels for 0% -> 7%
where the time goes in v1:
time: 139 us; the launch traced here: 138 us
  waiting for transfers between devices  72.1 us (52%)
  Pallas kernels  33.5 us (24%)
  starting transfers between devices  27.1 us (19%)
  local copies, waits for them, and re-layouts  4.66 us (3%)
    ppermute x5, waiting for transfers between devices, passed_along(): lax.ppermute(array, 'pair', [(i, (i + by) % length) for i in range(length)])  42.7 us
    ppermute x12, waiting for transfers between devices, along_y(): lax.ppermute(array, 'row', [(2 * y + h, 2 * ((y + by) % length) + h) for...  22.5 us
    ppermute x12, starting transfers between devices, along_y(): lax.ppermute(array, 'row', [(2 * y + h, 2 * ((y + by) % length) + h) for...  17.5 us
    pallas_call x7, Pallas kernels, rotated(): pl.pallas_call(apply_kernel, out_shape=jax.ShapeDtypeStruct((rows, W), F3...  13.8 us
    pallas_call x2, Pallas kernels, rotation(): pl.pallas_call(rotation_kernel, out_shape=[half, half], in_specs=[pl.Bloc...  13.4 us
    ppermute x2, waiting for transfers between devices, across_x(): lax.ppermute(array, 'row', [(i, i ^ 1) for i in range(lax.axis_size('row'...  6.94 us
    pallas_call x2, Pallas kernels, gram_pieces(): pl.pallas_call(gram_kernel, out_shape=[piece] * 4, grid_spec=pltpu.Prefet...  6.31 us
    ppermute x2, starting transfers between devices, across_x(): lax.ppermute(array, 'row', [(i, i ^ 1) for i in range(lax.axis_size('row'...  6.26 us
  transfers between devices with their start and end apart: 19, of which 17 were waited for; matrix products, arithmetic and copies ran while one was open for 0% of the time, Pallas kernels for 7%

profile of v1, /device:TPU:128, one launch (start us, length us, event | category | flops | bytes accessed | tf_op | source)
XLA Modules:
  0.0 138.3 jit_solution(16156442110204366530)
XLA Ops:
  3.8 3.2 %shard_map.41 = (f32[264,128]{1,0:T(8,128)S(1)}, f32[264,128]{1,0:T(8,128)S(1)}, f32[264,128]{1,0:T(8,128)S(1)}, f32[264,128]{1,0:T(8,128)S(1)}) custom-call(s32[1]{0:T(128)} %bitcast.where_ref, f32[2048,256]{1,0:T(8,128)S(1)} %copy-done, f32[2048,256]{1,0:T(8,128)S(1)} %copy-done.2), custom_call_target="tpu_custom_call" | custom-call | flops 1879048192 | bytes 4194304 | tf_op jit(solution)/shard_map/pallas_call | solution.py:89
  8.7 2.9 %collective-permute-start.1 = (f32[264,128]{1,0:T(8,128)S(1)}, f32[264,128]{1,0:T(8,128)S(1)}, u32[]{:S(2)}, u32[]{:S(2)}) collective-permute-start(f32[264,128]{1,0:T(8,128)S(1)} %get-tuple-element.16), channel_id=1, source_target_pairs={{0,128},{32,160},{64,192},{96,224},{128,0},{160,32},{192,64},{224,... | collective-permute-start | bytes 405512 | tf_op jit(solution)/shard_map/ppermute | solution.py:200
  13.7 4.1 %collective-permute-done.1 = f32[264,128]{1,0:T(8,128)S(1)} collective-permute-done((f32[264,128]{1,0:T(8,128)S(1)}, f32[264,128]{1,0:T(8,128)S(1)}, u32[]{:S(2)}, u32[]{:S(2)}) %collective-permute-start.1) | collective-permute-done | bytes 135200 | tf_op jit(solution)/shard_map/ppermute | solution.py:200
  17.8 3.1 %collective-permute-start.3 = (f32[264,128]{1,0:T(8,128)S(1)}, f32[264,128]{1,0:T(8,128)S(1)}, u32[]{:S(2)}, u32[]{:S(2)}) collective-permute-start(f32[264,128]{1,0:T(8,128)S(1)} %add_add_fusion.1), channel_id=1, source_target_pairs={{0,32},{32,0},{64,96},{96,64},{128,160},{160,128},{192,224},{224,1... | collective-permute-start | bytes 405512 | tf_op jit(solution)/shard_map/ppermute | solution.py:206
  20.9 3.5 %collective-permute-done.3 = f32[264,128]{1,0:T(8,128)S(1)} collective-permute-done((f32[264,128]{1,0:T(8,128)S(1)}, f32[264,128]{1,0:T(8,128)S(1)}, u32[]{:S(2)}, u32[]{:S(2)}) %collective-permute-start.3) | collective-permute-done | bytes 135200 | tf_op jit(solution)/shard_map/ppermute | solution.py:206
  24.5 2.2 %collective-permute-start.6 = (f32[264,128]{1,0:T(8,128)S(1)}, f32[264,128]{1,0:T(8,128)S(1)}, u32[]{:S(2)}, u32[]{:S(2)}) collective-permute-start(f32[264,128]{1,0:T(8,128)S(1)} %add.28.q0), channel_id=1, source_target_pairs={{0,192},{32,224},{64,0},{96,32},{128,64},{160,96},{192,128},{224,1... | collective-permute-start | bytes 405512 | tf_op jit(solution)/shard_map/ppermute | solution.py:200
  29.5 3.7 %collective-permute-done.5.q2 = f32[264,128]{1,0:T(8,128)S(1)} collective-permute-done((f32[264,128]{1,0:T(8,128)S(1)}, f32[264,128]{1,0:T(8,128)S(1)}, u32[]{:S(2)}, u32[]{:S(2)}) %collective-permute-start.5) | collective-permute-done | bytes 135200 | tf_op jit(solution)/shard_map/ppermute | solution.py:200
  34.7 6.7 %shard_map.42 = (bf16[512,512]{1,0:T(8,128)(2,1)S(1)}, bf16[512,512]{1,0:T(8,128)(2,1)S(1)}) custom-call(s32[1]{0:T(128)} %bitcast.where_ref, f32[264,128]{1,0:T(8,128)S(1)} %add.28.q0, f32[264,128]{1,0:T(8,128)S(1)} %collective-permute-done.4.q1, f32[264,128]{1,0:T(8,128)S(1)} %collective-permute-done.5.q2, f32[264,128]{1,0:T(8,128)S(1)} %collective-permute-done.6.q3), custom_call_target="tpu_custom_call" | custom-call | flops 4831838208 | bytes 2097152 | tf_op jit(solution)/shard_map/pallas_call | solution.py:161
  47.0 3.9 %shard_map.47.bottom_ref = f32[2048,256]{1,0:T(8,128)S(1)} custom-call(f32[2048,256]{1,0:T(8,128)S(1)} %copy-done.1, f32[2048,256]{1,0:T(8,128)} %bottom_ref.11, bf16[512,512]{1,0:T(8,128)(2,1)S(1)} %get-tuple-element.18.high_ref, bf16[512,512]{1,0:T(8,128)(2,1)S(1)} %get-tuple-element.19.low_ref), custom_call_target="tpu_custom_call" | custom-call | flops 1610612736 | bytes 6291456 | tf_op jit(solution)/shard_map/pallas_call | solution.py:182
  52.8 5.6 %collective-permute-done.8 = f32[512,256]{1,0:T(8,128)S(1)} collective-permute-done((f32[512,256]{1,0:T(8,128)S(1)}, f32[512,256]{1,0:T(8,128)S(1)}, u32[]{:S(2)}, u32[]{:S(2)}) %collective-permute-start.8) | collective-permute-done | bytes 524320 | tf_op jit(solution)/shard_map/ppermute | solution.py:195
  58.5 5.6 %collective-permute-done.9 = f32[512,256]{1,0:T(8,128)S(1)} collective-permute-done((f32[512,256]{1,0:T(8,128)S(1)}, f32[512,256]{1,0:T(8,128)S(1)}, u32[]{:S(2)}, u32[]{:S(2)}) %collective-permute-start.9) | collective-permute-done | bytes 524320 | tf_op jit(solution)/shard_map/ppermute | solution.py:195
  64.1 5.6 %collective-permute-done.10 = f32[512,256]{1,0:T(8,128)S(1)} collective-permute-done((f32[512,256]{1,0:T(8,128)S(1)}, f32[512,256]{1,0:T(8,128)S(1)}, u32[]{:S(2)}, u32[]{:S(2)}) %collective-permute-start.10) | collective-permute-done | bytes 524320 | tf_op jit(solution)/shard_map/ppermute | solution.py:195
  69.7 3.1 %shard_map.48 = (f32[264,128]{1,0:T(8,128)S(1)}, f32[264,128]{1,0:T(8,128)S(1)}, f32[264,128]{1,0:T(8,128)S(1)}, f32[264,128]{1,0:T(8,128)S(1)}) custom-call(s32[1]{0:T(128)} %bitcast.where_ref, f32[2048,256]{1,0:T(8,128)S(1)} %constant_dynamic-update-slice_fusion.top_ref, f32[2048,256]{1,0:T(8,128)S(1)} %shard_map.47.bottom_ref), custom_call_target="tpu_custom_call" | custom-call | flops 1879048192 | bytes 4194304 | tf_op jit(solution)/shard_map/pallas_call | solution.py:89
  72.9 2.0 %collective-permute-start.12 = (f32[264,128]{1,0:T(8,128)S(1)}, f32[264,128]{1,0:T(8,128)S(1)}, u32[]{:S(2)}, u32[]{:S(2)}) collective-permute-start(f32[264,128]{1,0:T(8,128)S(1)} %get-tuple-element.22), channel_id=1, source_target_pairs={{0,128},{32,160},{64,192},{96,224},{128,0},{160,32},{192,64},{224,... | collective-permute-start | bytes 405512 | tf_op jit(solution)/shard_map/ppermute | solution.py:200
  76.7 3.9 %collective-permute-done.11 = f32[264,128]{1,0:T(8,128)S(1)} collective-permute-done((f32[264,128]{1,0:T(8,128)S(1)}, f32[264,128]{1,0:T(8,128)S(1)}, u32[]{:S(2)}, u32[]{:S(2)}) %collective-permute-start.11) | collective-permute-done | bytes 135200 | tf_op jit(solution)/shard_map/ppermute | solution.py:200
  81.5 3.1 %collective-permute-start.14 = (f32[264,128]{1,0:T(8,128)S(1)}, f32[264,128]{1,0:T(8,128)S(1)}, u32[]{:S(2)}, u32[]{:S(2)}) collective-permute-start(f32[264,128]{1,0:T(8,128)S(1)} %add_add_fusion), channel_id=1, source_target_pairs={{0,32},{32,0},{64,96},{96,64},{128,160},{160,128},{192,224},{224,1... | collective-permute-start | bytes 405512 | tf_op jit(solution)/shard_map/ppermute | solution.py:206
  84.6 3.5 %collective-permute-done.14 = f32[264,128]{1,0:T(8,128)S(1)} collective-permute-done((f32[264,128]{1,0:T(8,128)S(1)}, f32[264,128]{1,0:T(8,128)S(1)}, u32[]{:S(2)}, u32[]{:S(2)}) %collective-permute-start.14) | collective-permute-done | bytes 135200 | tf_op jit(solution)/shard_map/ppermute | solution.py:206
  88.1 2.7 %collective-permute-start.17 = (f32[264,128]{1,0:T(8,128)S(1)}, f32[264,128]{1,0:T(8,128)S(1)}, u32[]{:S(2)}, u32[]{:S(2)}) collective-permute-start(f32[264,128]{1,0:T(8,128)S(1)} %add.32.q0), channel_id=1, source_target_pairs={{0,192},{32,224},{64,0},{96,32},{128,64},{160,96},{192,128},{224,1... | collective-permute-start | bytes 405512 | tf_op jit(solution)/shard_map/ppermute | solution.py:200
  91.8 3.1 %collective-permute-done.17.q3 = f32[264,128]{1,0:T(8,128)S(1)} collective-permute-done((f32[264,128]{1,0:T(8,128)S(1)}, f32[264,128]{1,0:T(8,128)S(1)}, u32[]{:S(2)}, u32[]{:S(2)}) %collective-permute-start.17) | collective-permute-done | bytes 135200 | tf_op jit(solution)/shard_map/ppermute | solution.py:200
  94.9 2.6 %collective-permute-done.16.q2 = f32[264,128]{1,0:T(8,128)S(1)} collective-permute-done((f32[264,128]{1,0:T(8,128)S(1)}, f32[264,128]{1,0:T(8,128)S(1)}, u32[]{:S(2)}, u32[]{:S(2)}) %collective-permute-start.16) | collective-permute-done | bytes 135200 | tf_op jit(solution)/shard_map/ppermute | solution.py:200
  98.5 6.7 %shard_map.49 = (bf16[512,512]{1,0:T(8,128)(2,1)S(1)}, bf16[512,512]{1,0:T(8,128)(2,1)S(1)}) custom-call(s32[1]{0:T(128)} %bitcast.where_ref, f32[264,128]{1,0:T(8,128)S(1)} %add.32.q0, f32[264,128]{1,0:T(8,128)S(1)} %collective-permute-done.15.q1, f32[264,128]{1,0:T(8,128)S(1)} %collective-permute-done.16.q2, f32[264,128]{1,0:T(8,128)S(1)} %collective-permute-done.17.q3), custom_call_target="tpu_custom_call" | custom-call | flops 4831838208 | bytes 2097152 | tf_op jit(solution)/shard_map/pallas_call | solution.py:161
  105.3 4.1 %shard_map.50 = f32[2048,256]{1,0:T(8,128)S(1)} custom-call(f32[2048,256]{1,0:T(8,128)S(1)} %constant_dynamic-update-slice_fusion.top_ref, f32[2048,256]{1,0:T(8,128)} %copy-done.4, bf16[512,512]{1,0:T(8,128)(2,1)S(1)} %get-tuple-element.24.high_ref, bf16[512,512]{1,0:T(8,128)(2,1)S(1)} %get-tuple-element.25.low_ref), custom_call_target="tpu_custom_call" | custom-call | flops 1610612736 | bytes 6291456 | tf_op jit(solution)/shard_map/pallas_call | solution.py:182
  109.5 3.4 %shard_map.51 = f32[2048,256]{1,0:T(8,128)} custom-call(f32[2048,256]{1,0:T(8,128)S(1)} %constant_dynamic-update-slice_fusion.top_ref, f32[2048,256]{1,0:T(8,128)S(1)} %copy-done.5, bf16[512,512]{1,0:T(8,128)(2,1)S(1)} %get-tuple-element.24.high_ref, bf16[512,512]{1,0:T(8,128)(2,1)S(1)} %get-tuple-element.25.low_ref), custom_call_target="tpu_custom_call" | custom-call | flops 1610612736 | bytes 6291456 | tf_op jit(solution)/shard_map/pallas_call | solution.py:182
  112.9 24.1 %collective-permute-done.18 = f32[2048,256]{1,0:T(8,128)S(1)} collective-permute-done((f32[2048,256]{1,0:T(8,128)S(1)}, f32[2048,256]{1,0:T(8,128)S(1)}, u32[]{:S(2)}, u32[]{:S(2)}) %collective-permute-start.18) | collective-permute-done | bytes 2097184 | tf_op jit(solution)/shard_map/ppermute | solution.py:195
  (46 shorter events, 25.0 us)
Async XLA Ops:
  0.6 1.6 %copy-start = (f32[2048,256]{1,0:T(8,128)S(1)}, f32[2048,256]{1,0:T(8,128)}, u32[]{:S(2)}) copy-start(f32[2048,256]{1,0:T(8,128)} %top_ref.11) | copy-start | bytes 6291460
  7.0 6.7 %collective-permute-start = (f32[264,128]{1,0:T(8,128)S(1)}, f32[264,128]{1,0:T(8,128)S(1)}, u32[]{:S(2)}, u32[]{:S(2)}) collective-permute-start(f32[264,128]{1,0:T(8,128)S(1)} %get-tuple-element.15), channel_id=1, source_target_pairs={{0,64},{32,96},{64,128},{96,160},{128,192},{160,224},{192,0},{224,... | collective-permute-start | bytes 405512 | tf_op jit(solution)/shard_map/ppermute | solution.py:200
  8.7 9.1 %collective-permute-start.1 = (f32[264,128]{1,0:T(8,128)S(1)}, f32[264,128]{1,0:T(8,128)S(1)}, u32[]{:S(2)}, u32[]{:S(2)}) collective-permute-start(f32[264,128]{1,0:T(8,128)S(1)} %get-tuple-element.16), channel_id=1, source_target_pairs={{0,128},{32,160},{64,192},{96,224},{128,0},{160,32},{192,64},{224,... | collective-permute-start | bytes 405512 | tf_op jit(solution)/shard_map/ppermute | solution.py:200
  11.6 6.2 %collective-permute-start.2 = (f32[264,128]{1,0:T(8,128)S(1)}, f32[264,128]{1,0:T(8,128)S(1)}, u32[]{:S(2)}, u32[]{:S(2)}) collective-permute-start(f32[264,128]{1,0:T(8,128)S(1)} %get-tuple-element.17), channel_id=1, source_target_pairs={{0,192},{32,224},{64,0},{96,32},{128,64},{160,96},{192,128},{224,1... | collective-permute-start | bytes 405512 | tf_op jit(solution)/shard_map/ppermute | solution.py:200
  17.8 6.6 %collective-permute-start.3 = (f32[264,128]{1,0:T(8,128)S(1)}, f32[264,128]{1,0:T(8,128)S(1)}, u32[]{:S(2)}, u32[]{:S(2)}) collective-permute-start(f32[264,128]{1,0:T(8,128)S(1)} %add_add_fusion.1), channel_id=1, source_target_pairs={{0,32},{32,0},{64,96},{96,64},{128,160},{160,128},{192,224},{224,1... | collective-permute-start | bytes 405512 | tf_op jit(solution)/shard_map/ppermute | solution.py:206
  24.4 17.0 %copy-start.1 = (f32[2048,256]{1,0:T(8,128)S(1)}, f32[2048,256]{1,0:T(8,128)}, u32[]{:S(2)}) copy-start(f32[2048,256]{1,0:T(8,128)} %top_ref.11) | copy-start | bytes 6291460
  24.4 16.9 %copy-start.3 = (f32[2048,256]{1,0:T(8,128)S(1)}, f32[2048,256]{1,0:T(8,128)}, u32[]{:S(2)}) copy-start(f32[2048,256]{1,0:T(8,128)} %bottom_ref.11) | copy-start | bytes 6291460
  24.5 5.1 %collective-permute-start.6 = (f32[264,128]{1,0:T(8,128)S(1)}, f32[264,128]{1,0:T(8,128)S(1)}, u32[]{:S(2)}, u32[]{:S(2)}) collective-permute-start(f32[264,128]{1,0:T(8,128)S(1)} %add.28.q0), channel_id=1, source_target_pairs={{0,192},{32,224},{64,0},{96,32},{128,64},{160,96},{192,128},{224,1... | collective-permute-start | bytes 405512 | tf_op jit(solution)/shard_map/ppermute | solution.py:200
  26.7 6.6 %collective-permute-start.5 = (f32[264,128]{1,0:T(8,128)S(1)}, f32[264,128]{1,0:T(8,128)S(1)}, u32[]{:S(2)}, u32[]{:S(2)}) collective-permute-start(f32[264,128]{1,0:T(8,128)S(1)} %add.28.q0), channel_id=1, source_target_pairs={{0,128},{32,160},{64,192},{96,224},{128,0},{160,32},{192,64},{224,... | collective-permute-start | bytes 405512 | tf_op jit(solution)/shard_map/ppermute | solution.py:200
  27.8 6.8 %collective-permute-start.4 = (f32[264,128]{1,0:T(8,128)S(1)}, f32[264,128]{1,0:T(8,128)S(1)}, u32[]{:S(2)}, u32[]{:S(2)}) collective-permute-start(f32[264,128]{1,0:T(8,128)S(1)} %add.28.q0), channel_id=1, source_target_pairs={{0,64},{32,96},{64,128},{96,160},{128,192},{160,224},{192,0},{224,... | collective-permute-start | bytes 405512 | tf_op jit(solution)/shard_map/ppermute | solution.py:200
  42.0 10.8 %collective-permute-start.7 = (f32[512,256]{1,0:T(8,128)S(1)}, f32[512,256]{1,0:T(8,128)S(1)}, u32[]{:S(2)}, u32[]{:S(2)}) collective-permute-start(f32[512,256]{1,0:T(8,128)S(1)} %shard_map.43), channel_id=1, source_target_pairs={{0,1},{1,2},{2,3},{3,4},{4,5},{5,6},{6,7},{7,8},{8,9},{9,10},{10,1... | collective-permute-start | bytes 1572872 | tf_op jit(solution)/shard_map/ppermute | solution.py:195
  42.7 15.7 %collective-permute-start.8 = (f32[512,256]{1,0:T(8,128)S(1)}, f32[512,256]{1,0:T(8,128)S(1)}, u32[]{:S(2)}, u32[]{:S(2)}) collective-permute-start(f32[512,256]{1,0:T(8,128)S(1)} %shard_map.44), channel_id=1, source_target_pairs={{0,1},{1,2},{2,3},{3,4},{4,5},{5,6},{6,7},{7,8},{8,9},{9,10},{10,1... | collective-permute-start | bytes 1572872 | tf_op jit(solution)/shard_map/ppermute | solution.py:195
  45.2 18.9 %collective-permute-start.9 = (f32[512,256]{1,0:T(8,128)S(1)}, f32[512,256]{1,0:T(8,128)S(1)}, u32[]{:S(2)}, u32[]{:S(2)}) collective-permute-start(f32[512,256]{1,0:T(8,128)S(1)} %shard_map.45), channel_id=1, source_target_pairs={{0,1},{1,2},{2,3},{3,4},{4,5},{5,6},{6,7},{7,8},{8,9},{9,10},{10,1... | collective-permute-start | bytes 1572872 | tf_op jit(solution)/shard_map/ppermute | solution.py:195
  45.9 23.8 %collective-permute-start.10 = (f32[512,256]{1,0:T(8,128)S(1)}, f32[512,256]{1,0:T(8,128)S(1)}, u32[]{:S(2)}, u32[]{:S(2)}) collective-permute-start(f32[512,256]{1,0:T(8,128)S(1)} %shard_map.46), channel_id=1, source_target_pairs={{0,1},{1,2},{2,3},{3,4},{4,5},{5,6},{6,7},{7,8},{8,9},{9,10},{10,1... | collective-permute-start | bytes 1572872 | tf_op jit(solution)/shard_map/ppermute | solution.py:195
  51.0 18.7 %copy-start.4 = (f32[2048,256]{1,0:T(8,128)}, f32[2048,256]{1,0:T(8,128)S(1)}, u32[]{:S(2)}) copy-start(f32[2048,256]{1,0:T(8,128)S(1)} %shard_map.47.bottom_ref) | copy-start | bytes 6291460
  72.8 7.7 %collective-permute-start.11 = (f32[264,128]{1,0:T(8,128)S(1)}, f32[264,128]{1,0:T(8,128)S(1)}, u32[]{:S(2)}, u32[]{:S(2)}) collective-permute-start(f32[264,128]{1,0:T(8,128)S(1)} %get-tuple-element.21), channel_id=1, source_target_pairs={{0,64},{32,96},{64,128},{96,160},{128,192},{160,224},{192,0},{224,... | collective-permute-start | bytes 405512 | tf_op jit(solution)/shard_map/ppermute | solution.py:200
  72.9 7.7 %collective-permute-start.12 = (f32[264,128]{1,0:T(8,128)S(1)}, f32[264,128]{1,0:T(8,128)S(1)}, u32[]{:S(2)}, u32[]{:S(2)}) collective-permute-start(f32[264,128]{1,0:T(8,128)S(1)} %get-tuple-element.22), channel_id=1, source_target_pairs={{0,128},{32,160},{64,192},{96,224},{128,0},{160,32},{192,64},{224,... | collective-permute-start | bytes 405512 | tf_op jit(solution)/shard_map/ppermute | solution.py:200
  74.9 6.5 %collective-permute-start.13 = (f32[264,128]{1,0:T(8,128)S(1)}, f32[264,128]{1,0:T(8,128)S(1)}, u32[]{:S(2)}, u32[]{:S(2)}) collective-permute-start(f32[264,128]{1,0:T(8,128)S(1)} %get-tuple-element.23), channel_id=1, source_target_pairs={{0,192},{32,224},{64,0},{96,32},{128,64},{160,96},{192,128},{224,1... | collective-permute-start | bytes 405512 | tf_op jit(solution)/shard_map/ppermute | solution.py:200
  81.5 6.6 %collective-permute-start.14 = (f32[264,128]{1,0:T(8,128)S(1)}, f32[264,128]{1,0:T(8,128)S(1)}, u32[]{:S(2)}, u32[]{:S(2)}) collective-permute-start(f32[264,128]{1,0:T(8,128)S(1)} %add_add_fusion), channel_id=1, source_target_pairs={{0,32},{32,0},{64,96},{96,64},{128,160},{160,128},{192,224},{224,1... | collective-permute-start | bytes 405512 | tf_op jit(solution)/shard_map/ppermute | solution.py:206
  88.1 6.8 %collective-permute-start.17 = (f32[264,128]{1,0:T(8,128)S(1)}, f32[264,128]{1,0:T(8,128)S(1)}, u32[]{:S(2)}, u32[]{:S(2)}) collective-permute-start(f32[264,128]{1,0:T(8,128)S(1)} %add.32.q0), channel_id=1, source_target_pairs={{0,192},{32,224},{64,0},{96,32},{128,64},{160,96},{192,128},{224,1... | collective-permute-start | bytes 405512 | tf_op jit(solution)/shard_map/ppermute | solution.py:200
  90.9 6.6 %collective-permute-start.16 = (f32[264,128]{1,0:T(8,128)S(1)}, f32[264,128]{1,0:T(8,128)S(1)}, u32[]{:S(2)}, u32[]{:S(2)}) collective-permute-start(f32[264,128]{1,0:T(8,128)S(1)} %add.32.q0), channel_id=1, source_target_pairs={{0,128},{32,160},{64,192},{96,224},{128,0},{160,32},{192,64},{224,... | collective-permute-start | bytes 405512 | tf_op jit(solution)/shard_map/ppermute | solution.py:200
  90.9 7.7 %collective-permute-start.15 = (f32[264,128]{1,0:T(8,128)S(1)}, f32[264,128]{1,0:T(8,128)S(1)}, u32[]{:S(2)}, u32[]{:S(2)}) collective-permute-start(f32[264,128]{1,0:T(8,128)S(1)} %add.32.q0), channel_id=1, source_target_pairs={{0,64},{32,96},{64,128},{96,160},{128,192},{160,224},{192,0},{224,... | collective-permute-start | bytes 405512 | tf_op jit(solution)/shard_map/ppermute | solution.py:200
  105.2 4.2 %copy-start.5 = (f32[2048,256]{1,0:T(8,128)S(1)}, f32[2048,256]{1,0:T(8,128)}, u32[]{:S(2)}) copy-start(f32[2048,256]{1,0:T(8,128)} %copy-done.4) | copy-start | bytes 6291460
  109.4 27.6 %collective-permute-start.18 = (f32[2048,256]{1,0:T(8,128)S(1)}, f32[2048,256]{1,0:T(8,128)S(1)}, u32[]{:S(2)}, u32[]{:S(2)}) collective-permute-start(f32[2048,256]{1,0:T(8,128)S(1)} %shard_map.50), channel_id=1, source_target_pairs={{0,1},{1,2},{2,3},{3,4},{4,5},{5,6},{6,7},{7,8},{8,9},{9,10},{10,1... | collective-permute-start | bytes 6291464 | tf_op jit(solution)/shard_map/ppermute | solution.py:195
  (1 other events, 1.6 us)
